TPU v7x, 256 devices: a whole 4x4x8 slice. The times are simulated.
256 devices in a mesh: seq: 128 (over y, z, x_lo, core), chan: 2 (over x_hi).
Axes of the slice: x: 4 (x_hi: 2, x_lo: 2; x = x_hi * 2 + x_lo), y: 4, z: 8, core: 2. Of those that a mesh axis runs over, the one named last changes fastest.
Arguments:
- inputs: bfloat16 [262144, 256], P('seq', 'chan'), may hold values from -6 to 6
- cotangent: bfloat16 [262144, 256], P('seq', 'chan'), may hold values from -18 to 18
- residues: float32 [16, 16], replicated, may hold values from -4 to 4
- decay_rates: float32 [16, 16], replicated, may hold values from 1.9073486e-06 to 0.0333333333
- skip_weight: float32 [256], P('chan'), may hold values from -4 to 4
Outputs:
- input_grad: bfloat16 [262144, 256], P('seq', 'chan')
- residue_grad: float32 [16, 16], replicated
- skip_grad: float32 [256], P('chan')
All inputs are finite; a program needn't handle non-finite values.
Results may differ from a plain program's by a relative error of at most 0.0012.
Values may be sent and summed in bfloat16 or wider, within the bound.
A program may use at most 64 MiB of HBM per device.

v0:
```python
import math
import jax
import jax.numpy as jnp
from jax import lax
from jax.sharding import PartitionSpec as P

GROUP = 16
BLOCK = 512
NG = 16
precise = lax.Precision.HIGHEST


def join_states(earlier, later):
    return (earlier[0] * later[0], later[1] + later[0] * earlier[1])


def block_work(packed):
    x_item, y_item, powers, tail_powers, coef_item = packed
    block_len = x_item.shape[0]
    filter_taps = jnp.dot(coef_item, powers, precision=precise)
    padded = jnp.concatenate([filter_taps, jnp.zeros((block_len,), jnp.float32)])
    repeated = jnp.tile(padded, block_len)[: block_len * (2 * block_len - 1)]
    toeplitz = repeated.reshape(block_len, 2 * block_len - 1)[:, :block_len]
    x_float = x_item.astype(jnp.float32)
    y_float = y_item.astype(jnp.float32)
    local_dx = jnp.dot(toeplitz, y_float, precision=precise)
    gram_matrix = jnp.dot(x_float, y_float.T, precision=precise)
    widened = jnp.concatenate(
        [gram_matrix, jnp.zeros((block_len, block_len - 1), jnp.float32)], axis=1
    )
    flattened = jnp.concatenate([widened.reshape(-1), jnp.zeros((block_len,), jnp.float32)])
    lag_sums = jnp.sum(flattened.reshape(block_len, 2 * block_len)[:, :block_len], axis=0)
    local_grad = jnp.dot(powers, lag_sums, precision=precise)
    summaries = jnp.dot(powers, y_float, precision=precise)
    tails_x = jnp.dot(tail_powers, x_float, precision=precise)
    return (local_dx, local_grad, summaries, tails_x)


def convolve_items(x_items, y_items, rate_items, coef_items, block_count, incoming_fn):
    block_len = x_items.shape[1]
    offsets = jnp.arange(block_len, dtype=jnp.float32)
    powers = jnp.exp(-rate_items[:, :, None] * offsets)
    tail_powers = jnp.exp(-rate_items[:, :, None] * (block_len - offsets))
    local_dx, local_grad, summaries, tails_x = lax.map(
        block_work, (x_items, y_items, powers, tail_powers, coef_items)
    )
    item_count, mode_count, col_count = summaries.shape
    per_block = col_count // block_count
    states = summaries.reshape(item_count, mode_count, block_count, per_block)
    step_decay = jnp.exp(-rate_items * block_len)[:, :, None]
    ordered = jnp.flip(jnp.moveaxis(states, 2, 0), 0)
    factors = jnp.broadcast_to(step_decay, ordered.shape)
    inclusive = lax.associative_scan(join_states, (factors, ordered))[1]
    inclusive = jnp.moveaxis(jnp.flip(inclusive, 0), 0, 2)
    device_decay = jnp.exp(-rate_items * (block_len * block_count))[:, :, None]
    incoming = incoming_fn(device_decay, inclusive[:, :, 0])
    remaining = (block_count - 1 - jnp.arange(block_count)).astype(jnp.float32)
    reach_decay = jnp.exp(-rate_items[:, :, None] * (block_len * remaining))[..., None]
    after_state = jnp.concatenate(
        [inclusive[:, :, 1:], jnp.zeros_like(inclusive[:, :, :1])], axis=2
    )
    after_state = (after_state + reach_decay * incoming[:, :, None, :]).reshape(
        item_count, mode_count, col_count
    )
    cross_dx = jnp.einsum(
        "ims,imc->isc", coef_items[:, :, None] * tail_powers, after_state, precision=precise
    )
    cross_grad = jnp.sum(tails_x * after_state, axis=2)
    return (local_dx + cross_dx, local_grad + cross_grad)


def no_carry(device_decay, device_total):
    return jnp.zeros_like(device_total)


def shards(inputs, cotangent, residues, decay_rates, skip_weight):
    tokens, width_dev = inputs.shape
    total_len = tokens * lax.axis_size("seq")
    mode_norm = jnp.sqrt(-jnp.expm1(-2.0 * decay_rates))
    mode_coefs = residues * mode_norm
    skip_partial = jnp.einsum(
        "tc,tc->c", inputs, cotangent, preferred_element_type=jnp.float32
    ) / math.sqrt(total_len)
    x_wide, y_wide = (
        lax.all_to_all(inputs, "seq", split_axis=1, concat_axis=0, tiled=True),
        lax.all_to_all(cotangent, "seq", split_axis=1, concat_axis=0, tiled=True),
    )
    chan_dev = x_wide.shape[1]
    full_blocks = total_len // BLOCK
    x_items = jnp.transpose(x_wide.reshape(full_blocks, BLOCK, chan_dev), (2, 1, 0))
    y_items = jnp.transpose(y_wide.reshape(full_blocks, BLOCK, chan_dev), (2, 1, 0))
    first_channel = lax.axis_index("seq") * chan_dev
    channel_ids = first_channel + jnp.arange(chan_dev, dtype=jnp.int32)
    selector = (channel_ids[:, None] % NG == jnp.arange(NG, dtype=jnp.int32)[None, :]).astype(
        jnp.float32
    )
    rate_items = jnp.dot(selector, decay_rates, precision=precise)
    coef_items = jnp.dot(selector, mode_coefs, precision=precise)
    skip_items = lax.dynamic_slice_in_dim(skip_weight, first_channel, chan_dev)
    mixed, grads = convolve_items(x_items, y_items, rate_items, coef_items, full_blocks, no_carry)
    dx_items = (mixed + skip_items[:, None, None] * y_items.astype(jnp.float32)).astype(
        jnp.bfloat16
    )
    dx_wide = jnp.transpose(dx_items, (2, 1, 0)).reshape(total_len, chan_dev)
    input_grad = lax.all_to_all(dx_wide, "seq", split_axis=0, concat_axis=1, tiled=True)
    group_grad = jnp.dot(selector.T, grads, precision=precise) * mode_norm
    group_grad = group_grad / math.sqrt(GROUP * total_len)
    group_grad, skip_grad = lax.psum((group_grad, skip_partial), "seq")
    group_grad = lax.psum(group_grad, "chan")
    return (input_grad, group_grad, skip_grad)


def solution(mesh):
    placed = (P("seq", "chan"), P("seq", "chan"), P(), P(), P("chan"))
    return jax.shard_map(
        shards,
        mesh=mesh,
        in_specs=placed,
        out_specs=(P("seq", "chan"), P(), P("chan")),
        check_vma=False,
    )
```

profile of v0, /device:TPU:4, one launch (start us, length us, event | category | flops | bytes accessed | tf_op | source)
XLA Modules:
  0.0 402.8 jit_solution(14199440599802911040)
XLA Ops:
  0.6 2.5 copy.48
  3.7 3.7 reduce.8
  7.3 1.2 reshape.387
  8.5 14.4 %all-to-all-start = ((bf16[128,2,1024]{2,1,0:T(2,128)(2,1)}), bf16[128,2,1024]{2,1,0:T(2,128)(2,1)S(1)}, u32[]{:S(2)}, u32[]{:S(2)}) async-start(bf16[128,2,1024]{2,1,0:T(2,128)(2,1)} %reshape.387), calls=%async_computation | async-start | bytes 1048576 | tf_op jit(solution)/shard_map/all_to_all | solution.py:86
  24.3 2.8 reshape.369
  28.2 3.7 reduce.10
  31.9 1.2 reshape.391
  34.1 7.9 %all-to-all-done = bf16[128,2,1024]{2,1,0:T(2,128)(2,1)S(1)} async-done(((bf16[128,2,1024]{2,1,0:T(2,128)(2,1)}), bf16[128,2,1024]{2,1,0:T(2,128)(2,1)S(1)}, u32[]{:S(2)}, u32[]{:S(2)}) %all-to-all-start) | async-done | bytes 524320 | tf_op jit(solution)/shard_map/all_to_all | solution.py:86
  42.0 6.4 %all-to-all-start.2 = ((bf16[128,2,1024]{2,1,0:T(2,128)(2,1)}), bf16[128,2,1024]{2,1,0:T(2,128)(2,1)S(1)}, u32[]{:S(2)}, u32[]{:S(2)}) async-start(bf16[128,2,1024]{2,1,0:T(2,128)(2,1)} %reshape.391), calls=%async_computation.2 | async-start | bytes 1048576 | tf_op jit(solution)/shard_map/all_to_all | solution.py:85
  48.9 3.0 bitcast_reduce_fusion.1
  53.0 1.4 copy.49
  66.9 1.7 fusion.3
  69.4 3.7 reduce.9
  73.0 1.2 reshape.389
  74.2 12.9 %all-to-all-start.1 = ((bf16[128,2,1024]{2,1,0:T(2,128)(2,1)}), bf16[128,2,1024]{2,1,0:T(2,128)(2,1)}, u32[]{:S(2)}, u32[]{:S(2)}) async-start(bf16[128,2,1024]{2,1,0:T(2,128)(2,1)} %reshape.389), calls=%async_computation.1 | async-start | bytes 1048576 | tf_op jit(solution)/shard_map/all_to_all | solution.py:105
  87.6 3.0 bitcast_reduce_fusion
  91.4 1.6 concatenate.49
  93.1 2.9 reshape.374
  96.0 1.5 concatenate.50
  97.5 1.7 reshape.375
  100.2 289.8 %all-reduce.22 = (f32[16,16]{1,0:T(8,128)S(1)}, f32[128]{0:T(128)}) all-reduce(f32[16,16]{1,0:T(8,128)S(1)} %multiply_multiply_fusion, f32[128]{0:T(128)S(1)} %broadcast_multiply_fusion.1), channel_id=1, replica_groups=mesh['seq'=128,'chan'=2] {'seq'}, use_global_device_ids=true, to_apply=%region_2.3 | all-reduce | flops 384 | bytes 3072 | tf_op jit(solution)/shard_map/psum | solution.py:108
  390.0 7.1 %psum.22 = f32[16,16]{1,0:T(8,128)} all-reduce(f32[16,16]{1,0:T(8,128)S(1)} %get-tuple-element.29), channel_id=1, replica_groups=mesh['seq'=128,'chan'=2] {'chan'}, use_global_device_ids=true, to_apply=%region_3.4 | all-reduce | flops 256 | bytes 2048 | tf_op jit(solution)/shard_map/psum | solution.py:109
  397.1 3.6 reshape.390
  400.7 1.9 copy.54
  (126 shorter events, 20.8 us)
Async XLA Ops:
  3.1 19.8 %copy-start.3 = (f32[16,16]{1,0:T(8,128)S(1)}, f32[16,16]{1,0:T(8,128)}, u32[]{:S(2)}) copy-start(f32[16,16]{1,0:T(8,128)} %param.8) | copy-start | bytes 3076
  3.1 20.0 %copy-start.4 = (f32[16,16]{1,0:T(8,128)S(1)}, f32[16,16]{1,0:T(8,128)}, u32[]{:S(2)}) copy-start(f32[16,16]{1,0:T(8,128)} %param.7) | copy-start | bytes 3076
  8.5 33.5 %all-to-all-start = ((bf16[128,2,1024]{2,1,0:T(2,128)(2,1)}), bf16[128,2,1024]{2,1,0:T(2,128)(2,1)S(1)}, u32[]{:S(2)}, u32[]{:S(2)}) async-start(bf16[128,2,1024]{2,1,0:T(2,128)(2,1)} %reshape.387), calls=%async_computation | async-start | bytes 1048576 | tf_op jit(solution)/shard_map/all_to_all | solution.py:86
  24.2 3.0 copy-start.2
  27.2 5.8 %copy-start.5 = (f32[128]{0:T(128)S(1)}, f32[128]{0:T(128)}, u32[]{:S(2)}) copy-start(f32[128]{0:T(128)} %param.9) | copy-start | bytes 1540
  27.2 6.4 %copy-start.1 = (bf16[2048,128]{1,0:T(8,128)(2,1)S(1)}, bf16[2048,128]{1,0:T(8,128)(2,1)}, u32[]{:S(2)}) copy-start(bf16[2048,128]{1,0:T(8,128)(2,1)} %param.6) | copy-start | bytes 1572868
  42.0 32.2 %all-to-all-start.2 = ((bf16[128,2,1024]{2,1,0:T(2,128)(2,1)}), bf16[128,2,1024]{2,1,0:T(2,128)(2,1)S(1)}, u32[]{:S(2)}, u32[]{:S(2)}) async-start(bf16[128,2,1024]{2,1,0:T(2,128)(2,1)} %reshape.391), calls=%async_computation.2 | async-start | bytes 1048576 | tf_op jit(solution)/shard_map/all_to_all | solution.py:85
  53.0 12.9 %copy-start = (f32[512,1023]{1,0:T(8,128)S(1)}, f32[512,1023]{1,0:T(8,128)}, u32[]{:S(2)}) copy-start(f32[512,1023]{1,0:T(8,128)} %reshape.369) | copy-start | bytes 6285316
  74.2 322.9 %all-to-all-start.1 = ((bf16[128,2,1024]{2,1,0:T(2,128)(2,1)}), bf16[128,2,1024]{2,1,0:T(2,128)(2,1)}, u32[]{:S(2)}, u32[]{:S(2)}) async-start(bf16[128,2,1024]{2,1,0:T(2,128)(2,1)} %reshape.389), calls=%async_computation.1 | async-start | bytes 1048576 | tf_op jit(solution)/shard_map/all_to_all | solution.py:105
where the time goes:
time: 408 us; the launch traced here: 403 us
  blocking collectives  297 us (73%)
  local copies, waits for them, and re-layouts  44.4 us (11%)
  starting transfers between devices  33.8 us (8%)
  other arithmetic  13.7 us (3%)
  waiting for transfers between devices  7.9 us (2%)
  matrix products  4.83 us (1%)
    psum x1, blocking collectives, shards(): group_grad, skip_grad = lax.psum((group_grad, skip_partial), 'seq')  290 us
    all_to_all x1, starting transfers between devices, shards(): lax.all_to_all(cotangent, 'seq', split_axis=1, concat_axis=0, tiled=True)  14.4 us
    all_to_all x1, starting transfers between devices, shards(): lax.all_to_all(dx_wide, 'seq', split_axis=0, concat_axis=1, tiled=True)  12.9 us
    unnamed x3, other arithmetic  11 us
    unnamed x22, local copies, waits for them, and re-layouts  9.43 us
  transfers between devices with their start and end apart: 3, of which 1 were waited for; matrix products, arithmetic and copies ran while one was open for 12% of the time, Pallas kernels for 0%

commit v1 on v0

--- a/solution.py
+++ b/solution.py
@@ -83,7 +83,12 @@
     ) / math.sqrt(total_len)
     x_wide, y_wide = (
         lax.all_to_all(inputs, "seq", split_axis=1, concat_axis=0, tiled=True),
-        lax.all_to_all(cotangent, "seq", split_axis=1, concat_axis=0, tiled=True),
+        jnp.concatenate(
+            lax.all_to_all(
+                jnp.stack(jnp.split(cotangent, lax.axis_size("seq"), axis=1)), "seq", 0, 0
+            ),
+            axis=0,
+        ),
     )
     chan_dev = x_wide.shape[1]
     full_blocks = total_len // BLOCK

time: 408 us -> 453 us (1.11)
  local copies, waits for them, and re-layouts: 44.4 us -> 91.3 us
    split x0 -> x7, local copies, waits for them, and re-layouts: none -> 45.7 us  [shards(): jnp.split(cotangent, lax.axis_size('seq'), axis=1)]
    unnamed x22 -> x150, local copies, waits for them, and re-layouts: 9.43 us -> 11.5 us
  transfers between devices with their start and end apart: 3 -> 3, of which waited for: 1 -> 1; matrix products, arithmetic and copies ran while one was open for 12% -> 11% of each run, Pallas kernels for 0% -> 0%
where the time goes in v1:
time: 453 us; the launch traced here: 449 us
  blocking collectives  297 us (66%)
  local copies, waits for them, and re-layouts  91.3 us (20%)
  starting transfers between devices  33.3 us (7%)
  other arithmetic  13.7 us (3%)
  waiting for transfers between devices  6.3 us (1%)
  matrix products  4.78 us (1%)
    psum x1, blocking collectives, shards(): group_grad, skip_grad = lax.psum((group_grad, skip_partial), 'seq')  290 us
    split x7, local copies, waits for them, and re-layouts, shards(): jnp.split(cotangent, lax.axis_size('seq'), axis=1)  45.7 us
    all_to_all x1, starting transfers between devices, shards(): lax.all_to_all(jnp.stack(jnp.split(cotangent, lax.axis_size('seq'), axis=...  14 us
    all_to_all x1, starting transfers between devices, shards(): lax.all_to_all(dx_wide, 'seq', split_axis=0, concat_axis=1, tiled=True)  12.9 us
    unnamed x150, local copies, waits for them, and re-layouts  11.5 us
    unnamed x3, other arithmetic  11 us
  transfers between devices with their start and end apart: 3, of which 1 were waited for; matrix products, arithmetic and copies ran while one was open for 11% of the time, Pallas kernels for 0%

profile of v1, /device:TPU:4, one launch (start us, length us, event | category | flops | bytes accessed | tf_op | source)
XLA Modules:
  0.0 448.5 jit_solution(13490783608067887817)
XLA Ops:
  0.6 8.9 %slice_reduce_fusion.116 = (bf16[2048]{0:T(1024)(128)(2,1)S(1)}, bf16[2048]{0:T(1024)(128)(2,1)S(1)}, bf16[2048]{0:T(1024)(128)(2,1)S(1)}, bf16[2048]{0:T(1024)(...) fusion(bf16[2048,128]{1,0:T(8,128)(2,1)} %param.6), kind=kLoop, calls=%fused_computation.140 | loop fusion | bytes 114688 | tf_op jit(solution)/shard_map/split | solution.py:88
  9.5 6.2 %slice_reduce_fusion.97 = (bf16[2048]{0:T(1024)(128)(2,1)S(1)}, bf16[2048]{0:T(1024)(128)(2,1)S(1)}, bf16[2048]{0:T(1024)(128)(2,1)S(1)}, bf16[2048]{0:T(1024)(1...) fusion(bf16[2048,128]{1,0:T(8,128)(2,1)S(1)} %copy-done), kind=kLoop, calls=%fused_computation.121 | loop fusion | bytes 155648 | tf_op jit(solution)/shard_map/split | solution.py:88
  15.8 6.0 %slice_reduce_fusion.78 = (bf16[2048]{0:T(1024)(128)(2,1)S(1)}, bf16[2048]{0:T(1024)(128)(2,1)S(1)}, bf16[2048]{0:T(1024)(128)(2,1)S(1)}, bf16[2048]{0:T(1024)(1...) fusion(bf16[2048,128]{1,0:T(8,128)(2,1)S(1)} %copy-done), kind=kLoop, calls=%fused_computation.102 | loop fusion | bytes 155648 | tf_op jit(solution)/shard_map/split | solution.py:88
  21.8 6.0 %slice_reduce_fusion.59 = (bf16[2048]{0:T(1024)(128)(2,1)S(1)}, bf16[2048]{0:T(1024)(128)(2,1)S(1)}, bf16[2048]{0:T(1024)(128)(2,1)S(1)}, bf16[2048]{0:T(1024)(1...) fusion(bf16[2048,128]{1,0:T(8,128)(2,1)S(1)} %copy-done), kind=kLoop, calls=%fused_computation.83 | loop fusion | bytes 155648 | tf_op jit(solution)/shard_map/split | solution.py:88
  27.9 6.0 %slice_reduce_fusion.40 = (bf16[2048]{0:T(1024)(128)(2,1)S(1)}, bf16[2048]{0:T(1024)(128)(2,1)S(1)}, bf16[2048]{0:T(1024)(128)(2,1)S(1)}, bf16[2048]{0:T(1024)(1...) fusion(bf16[2048,128]{1,0:T(8,128)(2,1)S(1)} %copy-done), kind=kLoop, calls=%fused_computation.64 | loop fusion | bytes 155648 | tf_op jit(solution)/shard_map/split | solution.py:88
  33.9 6.4 %slice_reduce_fusion.21 = (bf16[2048]{0:T(1024)(128)(2,1)S(1)}, bf16[2048]{0:T(1024)(128)(2,1)S(1)}, bf16[2048]{0:T(1024)(128)(2,1)S(1)}, bf16[2048]{0:T(1024)(1...) fusion(bf16[2048,128]{1,0:T(8,128)(2,1)S(1)} %copy-done), kind=kLoop, calls=%fused_computation.45 | loop fusion | bytes 155648 | tf_op jit(solution)/shard_map/split | solution.py:88
  40.4 6.0 %slice_reduce_fusion.1 = (bf16[2048]{0:T(1024)(128)(2,1)S(1)}, bf16[2048]{0:T(1024)(128)(2,1)S(1)}, bf16[2048]{0:T(1024)(128)(2,1)S(1)}, bf16[2048]{0:T(1024)(12...) fusion(bf16[2048,128]{1,0:T(8,128)(2,1)S(1)} %copy-done), kind=kLoop, calls=%fused_computation.25 | loop fusion | bytes 155648 | tf_op jit(solution)/shard_map/split | solution.py:88
  49.2 3.7 reduce.264
  54.1 14.0 %all-to-all-start = ((bf16[128,2,1024]{2,1,0:T(2,128)(2,1)}), bf16[128,2,1024]{2,1,0:T(2,128)(2,1)S(1)}, u32[]{:S(2)}, u32[]{:S(2)}) async-start(bf16[128,2,1024]{2,1,0:T(2,128)(2,1)} %reshape.508), calls=%async_computation | async-start | bytes 1048576 | tf_op jit(solution)/shard_map/all_to_all | solution.py:87
  69.4 2.8 reshape.362
  72.3 2.5 copy.62
  74.9 3.7 reduce.266
  80.8 6.3 %all-to-all-done = bf16[128,2,1024]{2,1,0:T(2,128)(2,1)S(1)} async-done(((bf16[128,2,1024]{2,1,0:T(2,128)(2,1)}), bf16[128,2,1024]{2,1,0:T(2,128)(2,1)S(1)}, u32[]{:S(2)}, u32[]{:S(2)}) %all-to-all-start) | async-done | bytes 524320 | tf_op jit(solution)/shard_map/all_to_all | solution.py:87
  87.1 6.4 %all-to-all-start.2 = ((bf16[128,2,1024]{2,1,0:T(2,128)(2,1)}), bf16[128,2,1024]{2,1,0:T(2,128)(2,1)S(1)}, u32[]{:S(2)}, u32[]{:S(2)}) async-start(bf16[128,2,1024]{2,1,0:T(2,128)(2,1)} %reshape.512), calls=%async_computation.2 | async-start | bytes 1048576 | tf_op jit(solution)/shard_map/all_to_all | solution.py:85
  94.0 3.0 bitcast_reduce_fusion.1
  114.6 3.7 reduce.265
  119.4 12.9 %all-to-all-start.1 = ((bf16[128,2,1024]{2,1,0:T(2,128)(2,1)}), bf16[128,2,1024]{2,1,0:T(2,128)(2,1)}, u32[]{:S(2)}, u32[]{:S(2)}) async-start(bf16[128,2,1024]{2,1,0:T(2,128)(2,1)} %reshape.510), calls=%async_computation.1 | async-start | bytes 1048576 | tf_op jit(solution)/shard_map/all_to_all | solution.py:110
  132.8 3.0 bitcast_reduce_fusion
  138.6 2.9 reshape.366
  143.0 1.7 reshape.367
  145.7 289.8 %all-reduce.22 = (f32[16,16]{1,0:T(8,128)S(1)}, f32[128]{0:T(128)}) all-reduce(f32[16,16]{1,0:T(8,128)S(1)} %multiply_multiply_fusion, f32[128]{0:T(128)S(1)} %broadcast_multiply_fusion.1), channel_id=1, replica_groups=mesh['seq'=128,'chan'=2] {'seq'}, use_global_device_ids=true, to_apply=%region_2.3 | all-reduce | flops 384 | bytes 3072 | tf_op jit(solution)/shard_map/psum | solution.py:113
  435.5 7.1 %psum.22 = f32[16,16]{1,0:T(8,128)} all-reduce(f32[16,16]{1,0:T(8,128)S(1)} %get-tuple-element.169), channel_id=1, replica_groups=mesh['seq'=128,'chan'=2] {'chan'}, use_global_device_ids=true, to_apply=%region_3.4 | all-reduce | flops 256 | bytes 2048 | tf_op jit(solution)/shard_map/psum | solution.py:114
  442.6 3.6 reshape.511
  446.2 1.9 copy.61
  (261 shorter events, 31.7 us)
Async XLA Ops:
  0.6 8.9 %copy-start = (bf16[2048,128]{1,0:T(8,128)(2,1)S(1)}, bf16[2048,128]{1,0:T(8,128)(2,1)}, u32[]{:S(2)}) copy-start(bf16[2048,128]{1,0:T(8,128)(2,1)} %param.6) | copy-start | bytes 1572868
  48.1 20.0 %copy-start.3 = (f32[16,16]{1,0:T(8,128)S(1)}, f32[16,16]{1,0:T(8,128)}, u32[]{:S(2)}) copy-start(f32[16,16]{1,0:T(8,128)} %param.8) | copy-start | bytes 3076
  48.1 20.1 %copy-start.4 = (f32[16,16]{1,0:T(8,128)S(1)}, f32[16,16]{1,0:T(8,128)}, u32[]{:S(2)}) copy-start(f32[16,16]{1,0:T(8,128)} %param.7) | copy-start | bytes 3076
  54.1 33.0 %all-to-all-start = ((bf16[128,2,1024]{2,1,0:T(2,128)(2,1)}), bf16[128,2,1024]{2,1,0:T(2,128)(2,1)S(1)}, u32[]{:S(2)}, u32[]{:S(2)}) async-start(bf16[128,2,1024]{2,1,0:T(2,128)(2,1)} %reshape.508), calls=%async_computation | async-start | bytes 1048576 | tf_op jit(solution)/shard_map/all_to_all | solution.py:87
  72.3 7.4 %copy-start.5 = (f32[128]{0:T(128)S(1)}, f32[128]{0:T(128)}, u32[]{:S(2)}) copy-start(f32[128]{0:T(128)} %param.9) | copy-start | bytes 1540
  72.3 8.0 %copy-start.2 = (bf16[2048,128]{1,0:T(8,128)(2,1)S(1)}, bf16[2048,128]{1,0:T(8,128)(2,1)}, u32[]{:S(2)}) copy-start(bf16[2048,128]{1,0:T(8,128)(2,1)} %param.5) | copy-start | bytes 1572868
  87.1 32.3 %all-to-all-start.2 = ((bf16[128,2,1024]{2,1,0:T(2,128)(2,1)}), bf16[128,2,1024]{2,1,0:T(2,128)(2,1)S(1)}, u32[]{:S(2)}, u32[]{:S(2)}) async-start(bf16[128,2,1024]{2,1,0:T(2,128)(2,1)} %reshape.512), calls=%async_computation.2 | async-start | bytes 1048576 | tf_op jit(solution)/shard_map/all_to_all | solution.py:85
  98.1 12.9 %copy-start.1 = (f32[512,1023]{1,0:T(8,128)S(1)}, f32[512,1023]{1,0:T(8,128)}, u32[]{:S(2)}) copy-start(f32[512,1023]{1,0:T(8,128)} %reshape.362) | copy-start | bytes 6285316
  119.4 323.2 %all-to-all-start.1 = ((bf16[128,2,1024]{2,1,0:T(2,128)(2,1)}), bf16[128,2,1024]{2,1,0:T(2,128)(2,1)}, u32[]{:S(2)}, u32[]{:S(2)}) async-start(bf16[128,2,1024]{2,1,0:T(2,128)(2,1)} %reshape.510), calls=%async_computation.1 | async-start | bytes 1048576 | tf_op jit(solution)/shard_map/all_to_all | solution.py:110
